TPU v7x, 32 devices: a whole 2x2x4 slice. The times are simulated.
32 devices in a mesh: dp: 16 (over z, x, core), tensor: 2 (over y).
Axes of the slice: x: 2, y: 2, z: 4, core: 2. Of those that a mesh axis runs over, the one named last changes fastest.
Arguments:
- inputs: bfloat16 [40960, 1024], P(('dp', 'tensor')), may hold values from -6 to 6
- teacher: bfloat16 [40960, 1024], P(('dp', 'tensor')), may hold values from -6 to 6
- lengths: int32 [128], replicated, may hold values from 200 to 320, as said below
- first_gain: float32 [1024], replicated, may hold values from 0.5 to 1.5
- first_shift: float32 [1024], replicated, may hold values from -0.2 to 0.2
- query_key_value_weight: bfloat16 [3, 1024, 1024], P(None, 'dp', 'tensor'), may hold values from -0.1875 to 0.1875
- heads_bias: float32 [2, 1024], P(None, 'tensor'), may hold values from -0.2 to 0.2
- merge_weight: bfloat16 [1024, 1024], P('dp', 'tensor'), may hold values from -1.5 to 1.5
- merge_bias: float32 [1024], replicated, may hold values from -0.6 to 0.6
- second_gain: float32 [1024], replicated, may hold values from 0.5 to 1.5
- second_shift: float32 [1024], replicated, may hold values from -0.6 to 0.6
- expand_weight: bfloat16 [1024, 4096], P('dp', 'tensor'), may hold values from -0.1875 to 0.1875
- expand_bias: float32 [4096], P('tensor'), may hold values from -0.6 to 0.6
- reduce_weight: bfloat16 [1024, 4096], P('dp', 'tensor'), may hold values from -0.09375 to 0.09375
- reduce_bias: float32 [1024], replicated, may hold values from -0.6 to 0.6
Outputs:
- loss_value: float32 [], replicated
- outputs: bfloat16 [40960, 1024], P(('dp', 'tensor'))
- inputs_grad: float32 [40960, 1024], P(('dp', 'tensor'))
- first_gain_grad: float32 [1024], replicated
- first_shift_grad: float32 [1024], replicated
- heads_weight_grad: float32 [3, 1024, 1024], P(None, 'dp', 'tensor')
- heads_bias_grad: float32 [2, 1024], P(None, 'tensor')
- merge_weight_grad: float32 [1024, 1024], P('dp', 'tensor')
- merge_bias_grad: float32 [1024], replicated
- second_gain_grad: float32 [1024], replicated
- second_shift_grad: float32 [1024], replicated
- expand_weight_grad: float32 [1024, 4096], P('dp', 'tensor')
- expand_bias_grad: float32 [4096], P('tensor')
- reduce_weight_grad: float32 [1024, 4096], P('dp', 'tensor')
- reduce_bias_grad: float32 [1024], replicated
Inputs may be any that keep to these rules, and one draw needn't show every extreme that they name: `lengths`: in every draw some image has all 320 slots valid.
All inputs are finite; a program needn't handle non-finite values.
Results may differ from a plain program's by a relative error of at most 0.0095.
Values may be sent and summed in bfloat16 or wider, within the bound.
A program may use at most 320 MiB of HBM per device.

v0:
```python
from functools import partial
import math
import jax
import jax.numpy as jnp
from jax import lax
from jax.sharding import PartitionSpec as P

HD = 64
SLOTS = 320
EPSILON = 1e-05
MASKED_SCORE = -1e30


def layer_norm(rows, gain, shift):
    centre = jnp.mean(rows, axis=-1, keepdims=True)
    centred = rows - centre
    spread = jnp.mean(centred * centred, axis=-1, keepdims=True)
    return centred * lax.rsqrt(spread + EPSILON) * gain + shift


def gather_rows(values):
    return lax.all_gather(values, "tensor", axis=0, tiled=True)


def reduce_rows(values):
    return lax.psum_scatter(values, "tensor", scatter_dimension=0, tiled=True)


def fetch_mixing(query_key_value_weight, merge_weight):
    return (
        lax.all_gather(query_key_value_weight, "dp", axis=1, tiled=True),
        lax.all_gather(merge_weight, "dp", axis=0, tiled=True),
    )


def fetch_feed(expand_weight, reduce_weight):
    return (
        lax.all_gather(expand_weight, "dp", axis=0, tiled=True),
        lax.all_gather(reduce_weight, "dp", axis=0, tiled=True),
    )


def masked_scores(query_heads, key_heads, key_valid, scale):
    raw_scores = (
        jnp.einsum("bqhe,bkhe->bhqk", query_heads, key_heads, preferred_element_type=jnp.float32)
        * scale
    )
    return jnp.where(key_valid[:, None, None, :], raw_scores, MASKED_SCORE)


def body(
    inputs,
    teacher,
    lengths,
    first_gain,
    first_shift,
    query_key_value_weight,
    heads_bias,
    merge_weight,
    merge_bias,
    second_gain,
    second_shift,
    expand_weight,
    expand_bias,
    reduce_weight,
    reduce_bias,
):
    local_rows = inputs.shape[0]
    group_rows = local_rows * lax.axis_size("tensor")
    images = group_rows // SLOTS
    local_width = query_key_value_weight.shape[2]
    local_heads = local_width // HD
    scale = 1.0 / math.sqrt(HD)
    mine = lax.dynamic_slice_in_dim(lengths, lax.axis_index("dp") * images, images)
    key_valid = jnp.arange(SLOTS, dtype=jnp.int32)[None, :] < mine[:, None]
    row_valid = lax.dynamic_slice_in_dim(
        key_valid.reshape(group_rows), lax.axis_index("tensor") * local_rows, local_rows
    )
    row_valid = row_valid.astype(jnp.float32)[:, None]
    count = jnp.sum(lengths).astype(jnp.float32)
    inputs_f = inputs.astype(jnp.float32)
    normalized_rows, first_back = jax.vjp(layer_norm, inputs_f, first_gain, first_shift)
    normed_b = normalized_rows.astype(jnp.bfloat16)
    normalized_complete = gather_rows(normed_b)
    heads_complete_rows, merge_full = fetch_mixing(query_key_value_weight, merge_weight)
    projected_heads = jnp.einsum(
        "xz,ezi->exi", normalized_complete, heads_complete_rows, preferred_element_type=jnp.float32
    )
    queries = (projected_heads[0] + heads_bias[0]).astype(jnp.bfloat16)
    key_rows = projected_heads[1].astype(jnp.bfloat16)
    value_rows = (projected_heads[2] + heads_bias[1]).astype(jnp.bfloat16)
    query_heads = queries.reshape(images, SLOTS, local_heads, HD)
    key_heads = key_rows.reshape(images, SLOTS, local_heads, HD)
    value_heads = value_rows.reshape(images, SLOTS, local_heads, HD)
    scores = masked_scores(query_heads, key_heads, key_valid, scale)
    highest = jnp.max(scores, axis=-1, keepdims=True)
    expo = jnp.exp(scores - highest)
    totals = jnp.sum(expo, axis=-1, keepdims=True)
    attend = expo / totals
    log_total = highest + jnp.log(totals)
    mixed = jnp.einsum(
        "bhqk,bkhe->bqhe",
        attend.astype(jnp.bfloat16),
        value_heads,
        preferred_element_type=jnp.float32,
    )
    mixed_b = mixed.reshape(group_rows, local_width).astype(jnp.bfloat16)
    branch_part = jnp.einsum("rf,df->rd", mixed_b, merge_full, preferred_element_type=jnp.float32)
    hidden_state = inputs_f + reduce_rows(branch_part) + merge_bias
    second, second_back = jax.vjp(layer_norm, hidden_state, second_gain, second_shift)
    second_b = second.astype(jnp.bfloat16)
    second_full = gather_rows(second_b)
    expand_full, reduce_full = fetch_feed(expand_weight, reduce_weight)
    pre_act = jnp.dot(second_full, expand_full, preferred_element_type=jnp.float32) + expand_bias
    activ, gelu_back = jax.vjp(partial(jax.nn.gelu, approximate=True), pre_act)
    activ_b = activ.astype(jnp.bfloat16)
    feed_part = jnp.einsum("rf,df->rd", activ_b, reduce_full, preferred_element_type=jnp.float32)
    feed_sum = reduce_rows(feed_part)
    result = (hidden_state + feed_sum + reduce_bias) * row_valid
    error = (result - teacher.astype(jnp.float32)) * row_valid
    loss_part = jnp.sum(error * error)
    result_grad = 2.0 * error / count
    expand_back, reduce_back = fetch_feed(expand_weight, reduce_weight)
    second_src = gather_rows(second_b)
    result_full = gather_rows(result_grad.astype(jnp.bfloat16))
    activ_grad = jnp.dot(result_full, reduce_back, preferred_element_type=jnp.float32)
    reduce_grad = jnp.einsum("rd,rf->df", result_full, activ_b, preferred_element_type=jnp.float32)
    pre_grad = gelu_back(activ_grad)[0].astype(jnp.bfloat16)
    expand_bias_grad = jnp.sum(pre_grad, axis=0, dtype=jnp.float32)
    expand_grad = jnp.einsum("rd,rf->df", second_src, pre_grad, preferred_element_type=jnp.float32)
    second_grad = reduce_rows(
        jnp.einsum("rf,df->rd", pre_grad, expand_back, preferred_element_type=jnp.float32)
    )
    hidden_ln_grad, second_gain_grad, second_shift_grad = second_back(second_grad)
    hidden_grad = result_grad + hidden_ln_grad
    reduce_bias_grad = jnp.sum(result_grad, axis=0)
    merge_bias_grad = jnp.sum(hidden_grad, axis=0)
    heads_pullback_rows, merge_back = fetch_mixing(query_key_value_weight, merge_weight)
    normalized_input_rows = gather_rows(normed_b)
    hidden_full = gather_rows(hidden_grad.astype(jnp.bfloat16))
    mixed_grad = jnp.einsum(
        "rd,df->rf", hidden_full, merge_back, preferred_element_type=jnp.float32
    ).astype(jnp.bfloat16)
    merge_grad = jnp.einsum("rd,rf->df", hidden_full, mixed_b, preferred_element_type=jnp.float32)
    mixed_heads = mixed_grad.reshape(images, SLOTS, local_heads, HD)
    attend_again = jnp.exp(masked_scores(query_heads, key_heads, key_valid, scale) - log_total)
    value_grad = jnp.einsum(
        "bhqk,bqhe->bkhe",
        attend_again.astype(jnp.bfloat16),
        mixed_heads,
        preferred_element_type=jnp.float32,
    ).astype(jnp.bfloat16)
    attend_grad = jnp.einsum(
        "bqhe,bkhe->bhqk", mixed_heads, value_heads, preferred_element_type=jnp.float32
    )
    score_grad = attend_again * (
        attend_grad - jnp.sum(attend_again * attend_grad, axis=-1, keepdims=True)
    )
    score_grad = score_grad.astype(jnp.bfloat16)
    query_grad = (
        jnp.einsum("bhqk,bkhe->bqhe", score_grad, key_heads, preferred_element_type=jnp.float32)
        * scale
    ).astype(jnp.bfloat16)
    key_grad = (
        jnp.einsum("bhqk,bqhe->bkhe", score_grad, query_heads, preferred_element_type=jnp.float32)
        * scale
    ).astype(jnp.bfloat16)
    projected_heads_gradient = jnp.stack(
        [
            query_grad.reshape(group_rows, local_width),
            key_grad.reshape(group_rows, local_width),
            value_grad.reshape(group_rows, local_width),
        ]
    )
    heads_bias_grad = jnp.stack(
        [
            jnp.sum(projected_heads_gradient[0], axis=0, dtype=jnp.float32),
            jnp.sum(projected_heads_gradient[2], axis=0, dtype=jnp.float32),
        ]
    )
    heads_grad = jnp.einsum(
        "jb,mjx->mbx",
        normalized_input_rows,
        projected_heads_gradient,
        preferred_element_type=jnp.float32,
    )
    normed_grad = reduce_rows(
        jnp.einsum(
            "mex,mwx->ew",
            projected_heads_gradient,
            heads_pullback_rows,
            preferred_element_type=jnp.float32,
        )
    )
    inputs_ln_grad, first_gain_grad, first_shift_grad = first_back(normed_grad)
    inputs_grad = hidden_grad + inputs_ln_grad
    heads_grad, merge_grad = (
        lax.psum_scatter(
            heads_grad.astype(jnp.bfloat16), "dp", scatter_dimension=1, tiled=True
        ).astype(jnp.float32),
        lax.psum_scatter(
            merge_grad.astype(jnp.bfloat16), "dp", scatter_dimension=0, tiled=True
        ).astype(jnp.float32),
    )
    expand_grad, reduce_grad = (
        lax.psum_scatter(
            expand_grad.astype(jnp.bfloat16), "dp", scatter_dimension=0, tiled=True
        ).astype(jnp.float32),
        lax.psum_scatter(
            reduce_grad.astype(jnp.bfloat16), "dp", scatter_dimension=0, tiled=True
        ).astype(jnp.float32),
    )
    heads_bias_grad, expand_bias_grad = lax.psum((heads_bias_grad, expand_bias_grad), "dp")
    summed = lax.psum(
        (
            first_gain_grad,
            first_shift_grad,
            second_gain_grad,
            second_shift_grad,
            merge_bias_grad,
            reduce_bias_grad,
            loss_part,
        ),
        ("dp", "tensor"),
    )
    loss_value = summed[6] / count
    return (
        loss_value,
        result.astype(jnp.bfloat16),
        inputs_grad,
        summed[0],
        summed[1],
        heads_grad,
        heads_bias_grad,
        merge_grad,
        summed[4],
        summed[2],
        summed[3],
        expand_grad,
        expand_bias_grad,
        reduce_grad,
        summed[5],
    )


def solution(mesh):
    return jax.shard_map(
        body,
        mesh=mesh,
        in_specs=(
            P(("dp", "tensor"), None),
            P(("dp", "tensor"), None),
            P(),
            P(),
            P(),
            P(None, "dp", "tensor"),
            P(None, "tensor"),
            P("dp", "tensor"),
            P(),
            P(),
            P(),
            P("dp", "tensor"),
            P("tensor"),
            P("dp", "tensor"),
            P(),
        ),
        out_specs=(
            P(),
            P(("dp", "tensor"), None),
            P(("dp", "tensor"), None),
            P(),
            P(),
            P(None, "dp", "tensor"),
            P(None, "tensor"),
            P("dp", "tensor"),
            P(),
            P(),
            P(),
            P("dp", "tensor"),
            P("tensor"),
            P("dp", "tensor"),
            P(),
        ),
        check_vma=False,
    )
```

profile of v0, /device:TPU:0, one launch (start us, length us, event | category | flops | bytes accessed | tf_op | source)
XLA Modules:
  0.0 1575.8 jit_solution(5867062736825207133)
XLA Ops:
  17.6 69.5 %all-gather.9.cloned.1.call-done = bf16[2560,1024]{1,0:T(8,128)(2,1)} async-done(((bf16[1280,1024]{1,0:T(8,128)(2,1)}), bf16[2560,1024]{1,0:T(8,128)(2,1)}) %all-gather.9.cloned.1.call-update) | async-done | bytes 5242896 | tf_op jit(solution)/shard_map/all_gather | solution.py:22
  87.2 47.4 %all-gather.11.cloned.1.call-done = bf16[3,1024,512]{2,1,0:T(8,128)(2,1)} async-done(((bf16[3,64,512]{2,1,0:T(8,128)(2,1)}), bf16[3,1024,512]{2,1,0:T(8,128)(2,1)}) %all-gather.11.cloned.1.call-update) | async-done | bytes 3145744 | tf_op jit(solution)/shard_map/all_gather | solution.py:31
  212.2 16.7 %fusion.13 = (f32[8,8,320]{2,1,0:T(8,128)S(1)}, f32[8,8,320,320]{2,3,1,0:T(8,128)}) fusion(pred[8,320]{1,0:T(8,128)(4,1)S(1)} %iota_compare_fusion, bf16[8,320,8,64]{1,3,2,0:T(8,128)(2,1)S(1)} %copy-done.6, bf16[8,320,8,64]{1,0,3,2:T(8,128)(2,1)} %add_convert_fusion), kind=kOutput, calls=%fused_computation.22 | convolution fusion | flops 858501120 | bytes 31541760 | tf_op jit(solution)/shard_map/bqhe,bkhe->bhqk/dot_general | solution.py:45
  243.0 16.4 %convert_bitcast_fusion.2 = bf16[8,320,8,64]{1,3,2,0:T(8,128)(2,1)} fusion(f32[8,8,320]{2,1,0:T(8,128)S(1)} %fusion, f32[8,8,320]{2,1,0:T(8,128)S(1)} %get-tuple-element.91, f32[8,8,320,320]{2,3,1,0:T(8,128)} %get-tuple-element.92, pred[8,320]{1,0:T(8,128)(4,1)S(1)} %iota_compare_fusion, bf16[8,320,8,64]{1,0,3,2:T(8,128)(2,1)} %add_convert_fusion.1), kind=kOutput, calls=%fused_computation.69 | convolution fusion | flops 872939520 | bytes 31623680 | tf_op jit(solution)/shard_map/bhqk,bkhe->bqhe/dot_general | solution.py:101
  280.4 120.2 %reduce-scatter.8.cloned.1.call-done = f32[1280,1024]{1,0:T(8,128)} async-done(((f32[2560,1024]{1,0:T(8,128)}), f32[1280,1024]{1,0:T(8,128)}) %reduce-scatter.8.cloned.1.call-update) | async-done | bytes 5242896 | tf_op jit(solution)/shard_map/reduce_scatter | solution.py:26
  409.3 43.9 %all-gather.17.cloned.1.call-done = bf16[1024,2048]{1,0:T(8,128)(2,1)} async-done(((bf16[64,2048]{1,0:T(8,128)(2,1)}), bf16[1024,2048]{1,0:T(8,128)(2,1)}) %all-gather.17.cloned.1.call-update) | async-done | bytes 4194320 | tf_op jit(solution)/shard_map/all_gather | solution.py:38
  453.2 69.1 %all-gather.15.cloned.1.call-done = bf16[2560,1024]{1,0:T(8,128)(2,1)} async-done(((bf16[1280,1024]{1,0:T(8,128)(2,1)}), bf16[2560,1024]{1,0:T(8,128)(2,1)}) %all-gather.15.cloned.1.call-update) | async-done | bytes 5242896 | tf_op jit(solution)/shard_map/all_gather | solution.py:22
  522.3 23.8 %multiply_convert_fusion.1 = (bf16[2560,2048]{1,0:T(8,128)(2,1)}, f32[2560,2048]{1,0:T(8,128)}) fusion(f32[2048]{0:T(1024)S(1)} %copy-done.43, bf16[2560,1024]{1,0:T(8,128)(2,1)} %all-gather.15.cloned.1.call-done, bf16[1024,2048]{1,0:T(8,128)(2,1)} %all-gather.17.cloned.1.call-done), kind=kOutput, calls=%fused_computation.18 | convolution fusion | flops 10789847040 | bytes 40902656 | tf_op jit(solution)/shard_map/dot_general | solution.py:114
  546.1 29.1 %all-gather.19.cloned.1.call-done = bf16[1024,2048]{1,0:T(8,128)(2,1)} async-done(((bf16[64,2048]{1,0:T(8,128)(2,1)}), bf16[1024,2048]{1,0:T(8,128)(2,1)}) %all-gather.19.cloned.1.call-update) | async-done | bytes 4194320 | tf_op jit(solution)/shard_map/all_gather | solution.py:39
  575.2 16.7 %fusion.62 = f32[2560,1024]{1,0:T(8,128)} fusion(bf16[2560,2048]{1,0:T(8,128)(2,1)} %get-tuple-element.93, bf16[1024,2048]{1,0:T(8,128)(2,1)} %all-gather.19.cloned.1.call-done), kind=kOutput, calls=%fused_computation.111 | convolution fusion | flops 10737418240 | bytes 25165824 | tf_op jit(solution)/shard_map/rf,df->rd/dot_general | solution.py:117
  594.0 118.4 %reduce-scatter.10.cloned.1.call-done = f32[1280,1024]{1,0:T(8,128)} async-done(((f32[2560,1024]{1,0:T(8,128)}), f32[1280,1024]{1,0:T(8,128)}) %reduce-scatter.10.cloned.1.call-update) | async-done | bytes 5242896 | tf_op jit(solution)/shard_map/reduce_scatter | solution.py:26
  726.7 68.7 %all-gather.21.cloned.1.call-done = bf16[2560,1024]{1,0:T(8,128)(2,1)} async-done(((bf16[1280,1024]{1,0:T(8,128)(2,1)}), bf16[2560,1024]{1,0:T(8,128)(2,1)}) %all-gather.21.cloned.1.call-update) | async-done | bytes 5242896 | tf_op jit(solution)/shard_map/all_gather | solution.py:22
  795.3 29.0 %convert_reduce_fusion = (f32[2048]{0:T(1024)}, bf16[2560,2048]{1,0:T(8,128)(2,1)S(1)}) fusion(f32[2560,2048]{1,0:T(8,128)} %get-tuple-element.94, f32[2048]{0:T(1024)S(1)} %copy-done.43, bf16[2560,1024]{1,0:T(8,128)(2,1)} %all-gather.21.cloned.1.call-done, bf16[1024,2048]{1,0:T(8,128)(2,1)} %all-gather.19.cloned.1.call-done), kind=kOutput, calls=%fused_computation.17 | convolution fusion | flops 10858002432 | bytes 40910848 | tf_op jit(solution)/shard_map/dot_general | solution.py:126
  842.8 122.0 %reduce-scatter.12.cloned.1.call-done = f32[1280,1024]{1,0:T(8,128)} async-done(((f32[2560,1024]{1,0:T(8,128)}), f32[1280,1024]{1,0:T(8,128)}) %reduce-scatter.12.cloned.1.call-update) | async-done | bytes 5242896 | tf_op jit(solution)/shard_map/reduce_scatter | solution.py:26
  980.0 17.0 %convolution_convert_fusion.1 = bf16[1024,2048]{1,0:T(8,128)(2,1)} fusion(bf16[2560,1024]{1,0:T(8,128)(2,1)} %all-gather.21.cloned.1.call-done, bf16[2560,2048]{1,0:T(8,128)(2,1)} %get-tuple-element.93), kind=kOutput, calls=%fused_computation.63 | convolution fusion | flops 10739515392 | bytes 19922944 | tf_op jit(solution)/shard_map/rd,rf->df/dot_general | solution.py:127
  997.2 16.8 %convolution_convert_fusion.2 = bf16[1024,2048]{1,0:T(8,128)(2,1)} fusion(bf16[2560,1024]{1,0:T(8,128)(2,1)} %all-gather.15.cloned.1.call-done, bf16[2560,2048]{1,0:T(8,128)(2,1)} %copy-done.47), kind=kOutput, calls=%fused_computation.64 | convolution fusion | flops 10739515392 | bytes 19922944 | tf_op jit(solution)/shard_map/rd,rf->df/dot_general | solution.py:130
  1014.3 34.4 %all-gather.23.cloned.1.call-done = bf16[2560,1024]{1,0:T(8,128)(2,1)} async-done(((bf16[1280,1024]{1,0:T(8,128)(2,1)}), bf16[2560,1024]{1,0:T(8,128)(2,1)}) %all-gather.23.cloned.1.call-update) | async-done | bytes 5242896 | tf_op jit(solution)/shard_map/all_gather | solution.py:22
  1066.1 24.7 %multiply_reduce_fusion = (f32[8,8,320]{2,1,0:T(8,128)S(1)}, f32[8,8,320,320]{2,3,1,0:T(8,128)}) fusion(f32[8,8,320]{2,1,0:T(8,128)S(1)} %log_add_fusion, f32[8,8,320,320]{2,3,1,0:T(8,128)} %get-tuple-element.92, pred[8,320]{1,0:T(8,128)(4,1)S(1)} %iota_compare_fusion, bf16[8,320,8,64]{1,3,2,0:T(8,128)(2,1)} %copy.76, bf16[8,320,8,64]{1,0,3,2:T(8,128)(2,1)S(1)} %copy-done.11), kind=kOutput, calls=%fused_computation.1 | convolution fusion | flops 871608320 | bytes 57838080 | tf_op jit(solution)/shard_map/bqhe,bkhe->bhqk/dot_general | solution.py:153
  1090.9 26.7 %multiply_convert_fusion = bf16[8,8,320,320]{2,3,1,0:T(8,128)(2,1)} fusion(f32[8,8,320,320]{2,3,1,0:T(8,128)} %get-tuple-element.96, f32[8,8,320]{2,1,0:T(8,128)S(1)} %get-tuple-element.95, f32[8,8,320]{2,1,0:T(8,128)S(1)} %log_add_fusion, f32[8,8,320,320]{2,3,1,0:T(8,128)} %get-tuple-element.92, pred[8,320]{1,0:T(8,128)(4,1)S(1)} %iota_compare_fusion), kind=kLoop, calls=%fused_computation | loop fusion | flops 39321600 | bytes 65702400 | tf_op jit(solution)/shard_map/convert_element_type | solution.py:159
  1244.4 61.5 %all-reduce.2 = (f32[2,512]{1,0:T(2,128)}, f32[2048]{0:T(1024)}) all-reduce(f32[2,512]{1,0:T(2,128)S(1)} %pad_maximum_fusion, f32[2048]{0:T(1024)S(1)} %copy-done.35), channel_id=1, replica_groups=mesh['dp'=16,'tensor'=2] {'dp'}, use_global_device_ids=true, to_apply=%region_25.26 | all-reduce | flops 3072 | bytes 24576 | tf_op jit(solution)/shard_map/psum | solution.py:213
  1305.9 24.2 %all-reduce.5.cloned.1.call-done = bf16[3,1024,512]{2,0,1:T(4,128)(2,1)} async-done(((bf16[3,1024,512]{2,0,1:T(4,128)(2,1)}), bf16[3,1024,512]{2,0,1:T(4,128)(2,1)}) %all-reduce.5.cloned.1.call-update) | async-done | bytes 3145744
  1332.0 58.4 %reduce-scatter.16.cloned.1.call-done = bf16[64,512]{1,0:T(8,128)(2,1)} async-done(((bf16[1024,512]{1,0:T(8,128)(2,1)}), bf16[64,512]{1,0:T(8,128)(2,1)}) %reduce-scatter.16.cloned.1.call-update) | async-done | bytes 65552 | tf_op jit(solution)/shard_map/reduce_scatter | solution.py:201
  1391.9 121.6 %reduce-scatter.14.cloned.1.call-done = f32[1280,1024]{1,0:T(8,128)} async-done(((f32[2560,1024]{1,0:T(8,128)}), f32[1280,1024]{1,0:T(8,128)}) %reduce-scatter.14.cloned.1.call-update) | async-done | bytes 5242896 | tf_op jit(solution)/shard_map/reduce_scatter | solution.py:26
  1520.6 40.2 %all-reduce.1 = (f32[]{:T(128)}, f32[1024]{0:T(1024)}, f32[1024]{0:T(1024)}, f32[1024]{0:T(1024)}, f32[1024]{0:T(1024)}, /*index=5*/f32[1024]{0:T(1024)}, f32[1024]{0:T(1024)}) all-reduce(f32[]{:T(128)} %get-tuple-element.90, f32[1024]{0:T(1024)S(1)} %get-tuple-element.62, ...), channel_id=1, replica_groups=mesh['dp'=16,'tensor'=2] {'dp','tensor'}, use_global_device_ids=true, to_apply=%region_9.10 | all-reduce | flops 6145 | bytes 49160 | tf_op jit(solution)/shard_map/psum | solution.py:214
  (218 shorter events, 341.4 us)
Async XLA Ops:
  7.2 80.0 %all-gather.9.cloned.1.call-start = ((), (), s32[]{:S(2)}) async-start(), calls=%async_computation.7 | async-start | bytes 7864320 | tf_op jit(solution)/shard_map/all_gather | solution.py:22
  15.8 118.8 %all-gather.11.cloned.1.call-start = ((), (), s32[]{:S(2)}) async-start(), calls=%async_computation.8 | async-start | bytes 3342336 | tf_op jit(solution)/shard_map/all_gather | solution.py:31
  16.5 254.4 %all-gather.13.cloned.1.call-start = ((), (), s32[]{:S(2)}) async-start(), calls=%async_computation.9 | async-start | bytes 1114112 | tf_op jit(solution)/shard_map/all_gather | solution.py:32
  17.2 383.4 %reduce-scatter.8.cloned.1.call-start = ((), (), s32[]{:S(2)}) async-start(), calls=%async_computation.10 | async-start | bytes 15728640 | tf_op jit(solution)/shard_map/reduce_scatter | solution.py:26
  279.7 120.9 %copy-start.37 = (f32[1024]{0:T(1024)S(1)}, f32[1024]{0:T(1024)}, u32[]{:S(2)}) copy-start(f32[1024]{0:T(1024)} %param.23) | copy-start | bytes 12292
  279.8 173.5 %all-gather.17.cloned.1.call-start = ((), (), s32[]{:S(2)}) async-start(), calls=%async_computation.12 | async-start | bytes 4456448 | tf_op jit(solution)/shard_map/all_gather | solution.py:38
  280.4 241.9 %all-gather.15.cloned.1.call-start = ((), (), s32[]{:S(2)}) async-start(), calls=%async_computation.11 | async-start | bytes 7864320 | tf_op jit(solution)/shard_map/all_gather | solution.py:22
  408.5 166.7 %all-gather.19.cloned.1.call-start = ((), (), s32[]{:S(2)}) async-start(), calls=%async_computation.13 | async-start | bytes 4456448 | tf_op jit(solution)/shard_map/all_gather | solution.py:39
  409.2 303.2 %reduce-scatter.10.cloned.1.call-start = ((), (), s32[]{:S(2)}) async-start(), calls=%async_computation.14 | async-start | bytes 15728640 | tf_op jit(solution)/shard_map/reduce_scatter | solution.py:26
  591.9 120.6 %copy-start.39 = (f32[1024]{0:T(1024)S(1)}, f32[1024]{0:T(1024)}, u32[]{:S(2)}) copy-start(f32[1024]{0:T(1024)} %param.29) | copy-start | bytes 12292
  591.9 203.4 %all-gather.21.cloned.1.call-start = ((), (), s32[]{:S(2)}) async-start(), calls=%async_computation.15 | async-start | bytes 7864320 | tf_op jit(solution)/shard_map/all_gather | solution.py:22
  594.0 124.8 %copy-start.16 = (bf16[1280,1024]{1,0:T(8,128)(2,1)S(1)}, bf16[1280,1024]{1,0:T(8,128)(2,1)}, u32[]{:S(2)}) copy-start(bf16[1280,1024]{1,0:T(8,128)(2,1)} %param.16) | copy-start | bytes 7864324
  726.6 238.1 %reduce-scatter.12.cloned.1.call-start = ((), (), s32[]{:S(2)}) async-start(), calls=%async_computation.16 | async-start | bytes 15728640 | tf_op jit(solution)/shard_map/reduce_scatter | solution.py:26
  842.7 206.0 %all-gather.23.cloned.1.call-start = ((), (), s32[]{:S(2)}) async-start(), calls=%async_computation.17 | async-start | bytes 7864320 | tf_op jit(solution)/shard_map/all_gather | solution.py:22
  980.0 260.6 %reduce-scatter.20.cloned.1.call-start = ((), (), s32[]{:S(2)}) async-start(), calls=%async_computation.21 | async-start | bytes 4456448 | tf_op jit(solution)/shard_map/reduce_scatter | solution.py:209
  997.1 245.3 %reduce-scatter.18.cloned.1.call-start = ((), (), s32[]{:S(2)}) async-start(), calls=%async_computation.20 | async-start | bytes 4456448 | tf_op jit(solution)/shard_map/reduce_scatter | solution.py:206
  1014.1 316.1 %all-reduce.5.cloned.1.call-start = ((), (), s32[]{:S(2)}) async-start(), calls=%async_computation.22 | async-start | bytes 8388608
  1218.0 172.4 %reduce-scatter.16.cloned.1.call-start = ((), (), s32[]{:S(2)}) async-start(), calls=%async_computation.19 | async-start | bytes 1114112 | tf_op jit(solution)/shard_map/reduce_scatter | solution.py:201
  1225.6 287.9 %reduce-scatter.14.cloned.1.call-start = ((), (), s32[]{:S(2)}) async-start(), calls=%async_computation.18 | async-start | bytes 15728640 | tf_op jit(solution)/shard_map/reduce_scatter | solution.py:26
  1238.7 274.8 %copy-start.2 = (bf16[1280,1024]{1,0:T(8,128)(2,1)S(1)}, bf16[1280,1024]{1,0:T(8,128)(2,1)}, u32[]{:S(2)}) copy-start(bf16[1280,1024]{1,0:T(8,128)(2,1)} %param.15) | copy-start | bytes 7864324
  1238.7 274.8 %copy-start.23 = (f32[1280]{0:T(1024)S(1)}, f32[1280]{0:T(1024)}, u32[]{:S(2)}) copy-start(f32[1280]{0:T(1024)} %copy-done.22) | copy-start | bytes 15364
  1238.7 274.8 %copy-start.29 = (f32[1024]{0:T(1024)S(1)}, f32[1024]{0:T(1024)}, u32[]{:S(2)}) copy-start(f32[1024]{0:T(1024)} %param.18) | copy-start | bytes 12292
  1242.4 275.0 %copy-start.27 = (f32[1280]{0:T(1024)S(1)}, f32[1280]{0:T(1024)}, u32[]{:S(2)}) copy-start(f32[1280]{0:T(1024)} %copy-done.26) | copy-start | bytes 15364
  1242.4 275.0 %copy-start.25 = (f32[1280]{0:T(1024)S(1)}, f32[1280]{0:T(1024)}, u32[]{:S(2)}) copy-start(f32[1280]{0:T(1024)} %copy-done.24) | copy-start | bytes 15364
  (44 other events, 409.0 us)
Sparse Core Ops, SparseCore 0:
  15.9 71.2 all-gather.8
  89.4 45.1 all-gather.10
  136.8 36.7 all-gather.12
  279.9 120.7 reduce-scatter.7
  402.7 50.5 all-gather.16
  455.2 67.0 all-gather.14
  524.5 50.7 all-gather.18
  592.0 120.3 reduce-scatter.9
  726.7 68.5 all-gather.20
  842.8 121.8 reduce-scatter.11
  980.1 68.5 all-gather.22
  1052.4 72.4 reduce-scatter.19
  1129.2 71.3 reduce-scatter.17
  1218.1 111.9 all-reduce.4
  1334.0 56.3 reduce-scatter.15
  1392.5 120.8 reduce-scatter.13
where the time goes:
time: 1590 us; the launch traced here: 1580 us
  waiting for transfers between devices  930 us (58%)
  matrix products  266 us (17%)
  local copies, waits for them, and re-layouts  154 us (10%)
  other arithmetic  105 us (7%)
  blocking collectives  102 us (6%)
  between operations  17.8 us (1%)
    reduce_scatter x4, waiting for transfers between devices, reduce_rows(): return lax.psum_scatter(values, 'tensor', scatter_dimension=0, tiled=True)  482 us
    all_gather x4, waiting for transfers between devices, gather_rows(): return lax.all_gather(values, 'tensor', axis=0, tiled=True)  242 us
    psum x1, blocking collectives, body(): lax.psum((heads_bias_grad, expand_bias_grad), 'dp')  61.5 us
    reduce_scatter x1, waiting for transfers between devices, body(): lax.psum_scatter(merge_grad.astype(jnp.bfloat16), 'dp', scatter_dimension...  58.4 us
    all_gather x1, waiting for transfers between devices, fetch_mixing(): lax.all_gather(query_key_value_weight, 'dp', axis=1, tiled=True)  47.4 us
    another operation x7, local copies, waits for them, and re-layouts, body(): jnp.stack([query_grad.reshape(group_rows, local_width), key_grad.reshape(...  44.8 us
    all_gather x1, waiting for transfers between devices, fetch_feed(): lax.all_gather(expand_weight, 'dp', axis=0, tiled=True)  43.9 us
    psum x1, blocking collectives, body(): lax.psum((first_gain_grad, first_shift_grad, second_gain_grad, second_shi...  40.2 us
  transfers between devices with their start and end apart: 16, of which 13 were waited for; matrix products, arithmetic and copies ran while one was open for 25% of the time, Pallas kernels for 0%

commit v1 on v0

--- a/solution.py
+++ b/solution.py
@@ -1,14 +1,34 @@
+import functools
 from functools import partial
 import math
 import jax
 import jax.numpy as jnp
 from jax import lax
 from jax.sharding import PartitionSpec as P
+from jax.lax import axis_index, axis_size, ppermute
 
 HD = 64
 SLOTS = 320
 EPSILON = 1e-05
 MASKED_SCORE = -1e30
+
+
+def cut_leaves(original, array_dim):
+    b_now = axis_size("dp")
+    r_now = axis_index("dp")
+    o_now, out_arr = (b_now, r_now)
+    later, local_next = (original, 1)
+    while local_next < o_now:
+        u1 = tuple(((nth, nth ^ local_next) for nth in range(o_now)))
+        u_next = ppermute(later, axis_name="dp", perm=u1)
+        new = jnp.concatenate([later, u_next], array_dim)
+        lower = jnp.concatenate([u_next, later], array_dim)
+        later = jnp.where(out_arr & local_next == 0, new, lower)
+        local_next = 2 * local_next
+    return later
+
+
+name_skins = functools.partial(cut_leaves, array_dim=1)
 
 
 def layer_norm(rows, gain, shift):
@@ -28,7 +48,7 @@
 
 def fetch_mixing(query_key_value_weight, merge_weight):
     return (
-        lax.all_gather(query_key_value_weight, "dp", axis=1, tiled=True),
+        name_skins(query_key_value_weight),
         lax.all_gather(merge_weight, "dp", axis=0, tiled=True),
     )
 

time: 1590 us -> 1550 us (0.975)
  local copies, waits for them, and re-layouts: 154 us -> 123 us
  waiting for transfers between devices: 930 us -> 906 us
  matrix products: 266 us -> 285 us
    ppermute x0 -> x4, waiting for transfers between devices: none -> 96.5 us  [cut_leaves(): u_next = ppermute(later, axis_name='dp', perm=u1)]
    all_gather x4, waiting for transfers between devices: 242 us -> 172 us  [gather_rows(): return lax.all_gather(values, 'tensor', axis=0, tiled=True)]
    all_gather x1 -> x0, waiting for transfers between devices: 47.4 us -> none  [fetch_mixing(): lax.all_gather(query_key_value_weight, 'dp', axis=1, tiled=True)]
  transfers between devices with their start and end apart: 16 -> 19, of which waited for: 13 -> 15; matrix products, arithmetic and copies ran while one was open for 25% -> 25% of each run, Pallas kernels for 0% -> 0%
where the time goes in v1:
time: 1550 us
  waiting for transfers between devices  906 us (58%)
  matrix products  285 us (18%)
  local copies, waits for them, and re-layouts  123 us (8%)
  other arithmetic  104 us (7%)
  blocking collectives  102 us (7%)
  between operations  17.9 us (1%)
    reduce_scatter x4, waiting for transfers between devices, reduce_rows(): return lax.psum_scatter(values, 'tensor', scatter_dimension=0, tiled=True)  484 us
    all_gather x4, waiting for transfers between devices, gather_rows(): return lax.all_gather(values, 'tensor', axis=0, tiled=True)  172 us
    ppermute x4, waiting for transfers between devices, cut_leaves(): u_next = ppermute(later, axis_name='dp', perm=u1)  96.5 us
    psum x1, blocking collectives, body(): lax.psum((heads_bias_grad, expand_bias_grad), 'dp')  61.5 us
    reduce_scatter x1, waiting for transfers between devices, body(): lax.psum_scatter(merge_grad.astype(jnp.bfloat16), 'dp', scatter_dimension...  58.4 us
    all_gather x1, waiting for transfers between devices, fetch_feed(): lax.all_gather(expand_weight, 'dp', axis=0, tiled=True)  44.1 us
    another operation x7, local copies, waits for them, and re-layouts, body(): jnp.stack([query_grad.reshape(group_rows, local_width), key_grad.reshape(...  42.9 us
    psum x1, blocking collectives, body(): lax.psum((first_gain_grad, first_shift_grad, second_gain_grad, second_shi...  40.2 us
  transfers between devices with their start and end apart: 19, of which 15 were waited for; matrix products, arithmetic and copies ran while one was open for 25% of the time, Pallas kernels for 0%

profile of v1, /device:TPU:0, one launch (start us, length us, event | category | flops | bytes accessed | tf_op | source)
XLA Modules:
  0.0 1547.3 jit_solution(7847326728689312768)
XLA Ops:
  32.5 17.3 %collective-permute-done.2 = bf16[3,256,512]{2,1,0:T(8,128)(2,1)} collective-permute-done((bf16[3,256,512]{2,1,0:T(8,128)(2,1)S(1)}, bf16[3,256,512]{2,1,0:T(8,128)(2,1)}, u32[]{:S(2)}, u32[]{:S(2)}) %collective-permute-start.2) | collective-permute-done | bytes 786464 | tf_op jit(solution)/shard_map/ppermute | solution.py:23
  56.4 68.6 %collective-permute-done.3 = bf16[3,512,512]{2,1,0:T(8,128)(2,1)} collective-permute-done((bf16[3,512,512]{2,1,0:T(8,128)(2,1)}, bf16[3,512,512]{2,1,0:T(8,128)(2,1)}, u32[]{:S(2)}, u32[]{:S(2)}) %collective-permute-start.3) | collective-permute-done | bytes 1572896 | tf_op jit(solution)/shard_map/ppermute | solution.py:23
  175.0 16.5 %fusion.13 = (f32[8,8,320]{2,1,0:T(8,128)S(1)}, f32[8,8,320,320]{2,3,1,0:T(8,128)}) fusion(pred[8,320]{1,0:T(8,128)(4,1)S(1)} %iota_compare_fusion, bf16[8,320,8,64]{1,0,3,2:T(8,128)(2,1)} %convert_element_type.127, f32[8,320,8,64]{1,0,3,2:T(8,128)} %squeeze.8, f32[8,64]{1,0:T(8,128)S(1)} %add.156), kind=kOutput, calls=%fused_computation.22 | convolution fusion | flops 861122560 | bytes 34165248 | tf_op jit(solution)/shard_map/bqhe,bkhe->bhqk/dot_general | solution.py:65
  205.7 17.5 %convert_bitcast_fusion.2 = bf16[8,320,8,64]{1,3,2,0:T(8,128)(2,1)} fusion(f32[8,8,320]{2,1,0:T(8,128)S(1)} %fusion, f32[8,8,320]{2,1,0:T(8,128)S(1)} %get-tuple-element.91, f32[8,8,320,320]{2,3,1,0:T(8,128)} %get-tuple-element.92, pred[8,320]{1,0:T(8,128)(4,1)S(1)} %iota_compare_fusion, f32[8,320,8,64]{1,0,3,2:T(8,128)} %squeeze.7, f32[8,64]{1,0:T(8,128)S(1)} %add.152), kind=kOutput, calls=%fused_computation.72 | convolution fusion | flops 875560960 | bytes 34247168 | tf_op jit(solution)/shard_map/bhqk,bkhe->bqhe/dot_general | solution.py:121
  244.2 121.9 %reduce-scatter.8.cloned.1.call-done = f32[1280,1024]{1,0:T(8,128)} async-done(((f32[2560,1024]{1,0:T(8,128)}), f32[1280,1024]{1,0:T(8,128)}) %reduce-scatter.8.cloned.1.call-update) | async-done | bytes 5242896 | tf_op jit(solution)/shard_map/reduce_scatter | solution.py:46
  374.6 44.1 %all-gather.14.cloned.1.call-done = bf16[1024,2048]{1,0:T(8,128)(2,1)} async-done(((bf16[64,2048]{1,0:T(8,128)(2,1)}), bf16[1024,2048]{1,0:T(8,128)(2,1)}) %all-gather.14.cloned.1.call-update) | async-done | bytes 4194320 | tf_op jit(solution)/shard_map/all_gather | solution.py:58
  418.7 69.1 %all-gather.12.cloned.1.call-done = bf16[2560,1024]{1,0:T(8,128)(2,1)} async-done(((bf16[1280,1024]{1,0:T(8,128)(2,1)}), bf16[2560,1024]{1,0:T(8,128)(2,1)}) %all-gather.12.cloned.1.call-update) | async-done | bytes 5242896 | tf_op jit(solution)/shard_map/all_gather | solution.py:42
  487.8 23.8 %multiply_convert_fusion.1 = (bf16[2560,2048]{1,0:T(8,128)(2,1)}, f32[2560,2048]{1,0:T(8,128)}) fusion(f32[2048]{0:T(1024)S(1)} %copy-done.42, bf16[2560,1024]{1,0:T(8,128)(2,1)} %all-gather.12.cloned.1.call-done, bf16[1024,2048]{1,0:T(8,128)(2,1)} %all-gather.14.cloned.1.call-done), kind=kOutput, calls=%fused_computation.18 | convolution fusion | flops 10789847040 | bytes 40902656 | tf_op jit(solution)/shard_map/dot_general | solution.py:134
  511.6 28.8 %all-gather.16.cloned.1.call-done = bf16[1024,2048]{1,0:T(8,128)(2,1)} async-done(((bf16[64,2048]{1,0:T(8,128)(2,1)}), bf16[1024,2048]{1,0:T(8,128)(2,1)}) %all-gather.16.cloned.1.call-update) | async-done | bytes 4194320 | tf_op jit(solution)/shard_map/all_gather | solution.py:59
  540.4 16.6 %fusion.66 = f32[2560,1024]{1,0:T(8,128)} fusion(bf16[2560,2048]{1,0:T(8,128)(2,1)} %get-tuple-element.93, bf16[1024,2048]{1,0:T(8,128)(2,1)} %all-gather.16.cloned.1.call-done), kind=kOutput, calls=%fused_computation.117 | convolution fusion | flops 10737418240 | bytes 25165824 | tf_op jit(solution)/shard_map/rf,df->rd/dot_general | solution.py:137
  559.1 118.4 %reduce-scatter.10.cloned.1.call-done = f32[1280,1024]{1,0:T(8,128)} async-done(((f32[2560,1024]{1,0:T(8,128)}), f32[1280,1024]{1,0:T(8,128)}) %reduce-scatter.10.cloned.1.call-update) | async-done | bytes 5242896 | tf_op jit(solution)/shard_map/reduce_scatter | solution.py:46
  691.6 68.7 %all-gather.18.cloned.1.call-done = bf16[2560,1024]{1,0:T(8,128)(2,1)} async-done(((bf16[1280,1024]{1,0:T(8,128)(2,1)}), bf16[2560,1024]{1,0:T(8,128)(2,1)}) %all-gather.18.cloned.1.call-update) | async-done | bytes 5242896 | tf_op jit(solution)/shard_map/all_gather | solution.py:42
  760.2 28.8 %convert_reduce_fusion = (f32[2048]{0:T(1024)}, bf16[2560,2048]{1,0:T(8,128)(2,1)S(1)}) fusion(f32[2560,2048]{1,0:T(8,128)} %get-tuple-element.94, f32[2048]{0:T(1024)S(1)} %copy-done.42, bf16[2560,1024]{1,0:T(8,128)(2,1)} %all-gather.18.cloned.1.call-done, bf16[1024,2048]{1,0:T(8,128)(2,1)} %all-gather.16.cloned.1.call-done), kind=kOutput, calls=%fused_computation.17 | convolution fusion | flops 10858002432 | bytes 40910848 | tf_op jit(solution)/shard_map/dot_general | solution.py:146
  807.3 122.0 %reduce-scatter.12.cloned.1.call-done = f32[1280,1024]{1,0:T(8,128)} async-done(((f32[2560,1024]{1,0:T(8,128)}), f32[1280,1024]{1,0:T(8,128)}) %reduce-scatter.12.cloned.1.call-update) | async-done | bytes 5242896 | tf_op jit(solution)/shard_map/reduce_scatter | solution.py:46
  944.5 17.1 %convolution_convert_fusion.1 = bf16[1024,2048]{1,0:T(8,128)(2,1)} fusion(bf16[2560,1024]{1,0:T(8,128)(2,1)} %all-gather.18.cloned.1.call-done, bf16[2560,2048]{1,0:T(8,128)(2,1)} %get-tuple-element.93), kind=kOutput, calls=%fused_computation.65 | convolution fusion | flops 10739515392 | bytes 19922944 | tf_op jit(solution)/shard_map/rd,rf->df/dot_general | solution.py:147
  961.8 16.9 %convolution_convert_fusion.2 = bf16[1024,2048]{1,0:T(8,128)(2,1)} fusion(bf16[2560,1024]{1,0:T(8,128)(2,1)} %all-gather.12.cloned.1.call-done, bf16[2560,2048]{1,0:T(8,128)(2,1)} %copy-done.46), kind=kOutput, calls=%fused_computation.66 | convolution fusion | flops 10739515392 | bytes 19922944 | tf_op jit(solution)/shard_map/rd,rf->df/dot_general | solution.py:150
  978.7 34.5 %all-gather.20.cloned.1.call-done = bf16[2560,1024]{1,0:T(8,128)(2,1)} async-done(((bf16[1280,1024]{1,0:T(8,128)(2,1)}), bf16[2560,1024]{1,0:T(8,128)(2,1)}) %all-gather.20.cloned.1.call-update) | async-done | bytes 5242896 | tf_op jit(solution)/shard_map/all_gather | solution.py:42
  1029.8 32.4 %multiply_reduce_fusion = (f32[8,8,320]{2,1,0:T(8,128)S(1)}, f32[8,8,320,320]{2,3,1,0:T(8,128)}) fusion(f32[8,8,320]{2,1,0:T(8,128)S(1)} %log_add_fusion, f32[8,8,320,320]{2,3,1,0:T(8,128)} %get-tuple-element.92, pred[8,320]{1,0:T(8,128)(4,1)S(1)} %iota_compare_fusion, bf16[8,320,8,64]{1,3,2,0:T(8,128)(2,1)S(1)} %copy.71, f32[8,320,8,64]{1,0,3,2:T(8,128)} %squeeze.7, ...), kind=kOutput, calls=%fused_computation.1 | convolution fusion | flops 874229760 | bytes 60461568 | tf_op jit(solution)/shard_map/bqhe,bkhe->bhqk/dot_general | solution.py:173
  1062.1 26.6 %multiply_convert_fusion = bf16[8,8,320,320]{2,3,1,0:T(8,128)(2,1)} fusion(f32[8,8,320,320]{2,3,1,0:T(8,128)} %get-tuple-element.96, f32[8,8,320]{2,1,0:T(8,128)S(1)} %get-tuple-element.95, f32[8,8,320]{2,1,0:T(8,128)S(1)} %log_add_fusion, f32[8,8,320,320]{2,3,1,0:T(8,128)} %get-tuple-element.92, pred[8,320]{1,0:T(8,128)(4,1)S(1)} %iota_compare_fusion), kind=kLoop, calls=%fused_computation | loop fusion | flops 39321600 | bytes 65702400 | tf_op jit(solution)/shard_map/convert_element_type | solution.py:179
  1218.9 61.5 %all-reduce.2 = (f32[2,512]{1,0:T(2,128)}, f32[2048]{0:T(1024)}) all-reduce(f32[2,512]{1,0:T(2,128)S(1)} %pad_maximum_fusion, f32[2048]{0:T(1024)S(1)} %copy-done.35), channel_id=1, replica_groups=mesh['dp'=16,'tensor'=2] {'dp'}, use_global_device_ids=true, to_apply=%region_25.26 | all-reduce | flops 3072 | bytes 24576 | tf_op jit(solution)/shard_map/psum | solution.py:233
  1280.4 21.1 %all-reduce.5.cloned.1.call-done = bf16[3,1024,512]{2,0,1:T(4,128)(2,1)} async-done(((bf16[3,1024,512]{2,0,1:T(4,128)(2,1)}), bf16[3,1024,512]{2,0,1:T(4,128)(2,1)}) %all-reduce.5.cloned.1.call-update) | async-done | bytes 3145744
  1303.4 58.4 %reduce-scatter.16.cloned.1.call-done = bf16[64,512]{1,0:T(8,128)(2,1)} async-done(((bf16[1024,512]{1,0:T(8,128)(2,1)}), bf16[64,512]{1,0:T(8,128)(2,1)}) %reduce-scatter.16.cloned.1.call-update) | async-done | bytes 65552 | tf_op jit(solution)/shard_map/reduce_scatter | solution.py:221
  1363.3 121.6 %reduce-scatter.14.cloned.1.call-done = f32[1280,1024]{1,0:T(8,128)} async-done(((f32[2560,1024]{1,0:T(8,128)}), f32[1280,1024]{1,0:T(8,128)}) %reduce-scatter.14.cloned.1.call-update) | async-done | bytes 5242896 | tf_op jit(solution)/shard_map/reduce_scatter | solution.py:46
  1492.0 40.2 %all-reduce.1 = (f32[]{:T(128)}, f32[1024]{0:T(1024)}, f32[1024]{0:T(1024)}, f32[1024]{0:T(1024)}, f32[1024]{0:T(1024)}, /*index=5*/f32[1024]{0:T(1024)}, f32[1024]{0:T(1024)}) all-reduce(f32[]{:T(128)} %get-tuple-element.90, f32[1024]{0:T(1024)S(1)} %get-tuple-element.62, ...), channel_id=1, replica_groups=mesh['dp'=16,'tensor'=2] {'dp','tensor'}, use_global_device_ids=true, to_apply=%region_9.10 | all-reduce | flops 6145 | bytes 49160 | tf_op jit(solution)/shard_map/psum | solution.py:234
  (214 shorter events, 337.2 us)
Async XLA Ops:
  7.2 117.8 %all-gather.8.cloned.1.call-start = ((), (), s32[]{:S(2)}) async-start(), calls=%async_computation.7 | async-start | bytes 7864320 | tf_op jit(solution)/shard_map/all_gather | solution.py:42
  14.6 219.9 %all-gather.10.cloned.1.call-start = ((), (), s32[]{:S(2)}) async-start(), calls=%async_computation.8 | async-start | bytes 1114112 | tf_op jit(solution)/shard_map/all_gather | solution.py:52
  14.7 1.6 collective-permute-start
  16.4 12.4 collective-permute-start.1
  30.6 19.2 %collective-permute-start.2 = (bf16[3,256,512]{2,1,0:T(8,128)(2,1)S(1)}, bf16[3,256,512]{2,1,0:T(8,128)(2,1)}, u32[]{:S(2)}, u32[]{:S(2)}) collective-permute-start(bf16[3,256,512]{2,1,0:T(8,128)(2,1)S(1)} %maximum_select_fusion.2), channel_id=1, source_target_pairs={{0,8},{2,10},{4,12},{6,14},{8,0},{10,2},{12,4},{14,6},{16,24},{18,... | collective-permute-start | bytes 2359304 | tf_op jit(solution)/shard_map/ppermute | solution.py:23
  52.9 72.0 %collective-permute-start.3 = (bf16[3,512,512]{2,1,0:T(8,128)(2,1)}, bf16[3,512,512]{2,1,0:T(8,128)(2,1)}, u32[]{:S(2)}, u32[]{:S(2)}) collective-permute-start(bf16[3,512,512]{2,1,0:T(8,128)(2,1)} %maximum_select_fusion.1), channel_id=1, source_target_pairs={{0,16},{2,18},{4,20},{6,22},{8,24},{10,26},{12,28},{14,30},{16,0},... | collective-permute-start | bytes 4718600 | tf_op jit(solution)/shard_map/ppermute | solution.py:23
  55.4 310.7 %reduce-scatter.8.cloned.1.call-start = ((), (), s32[]{:S(2)}) async-start(), calls=%async_computation.9 | async-start | bytes 15728640 | tf_op jit(solution)/shard_map/reduce_scatter | solution.py:46
  243.4 175.3 %all-gather.14.cloned.1.call-start = ((), (), s32[]{:S(2)}) async-start(), calls=%async_computation.11 | async-start | bytes 4456448 | tf_op jit(solution)/shard_map/all_gather | solution.py:58
  244.0 243.8 %all-gather.12.cloned.1.call-start = ((), (), s32[]{:S(2)}) async-start(), calls=%async_computation.10 | async-start | bytes 7864320 | tf_op jit(solution)/shard_map/all_gather | solution.py:42
  374.0 166.4 %all-gather.16.cloned.1.call-start = ((), (), s32[]{:S(2)}) async-start(), calls=%async_computation.12 | async-start | bytes 4456448 | tf_op jit(solution)/shard_map/all_gather | solution.py:59
  374.5 303.0 %reduce-scatter.10.cloned.1.call-start = ((), (), s32[]{:S(2)}) async-start(), calls=%async_computation.13 | async-start | bytes 15728640 | tf_op jit(solution)/shard_map/reduce_scatter | solution.py:46
  557.0 203.2 %all-gather.18.cloned.1.call-start = ((), (), s32[]{:S(2)}) async-start(), calls=%async_computation.14 | async-start | bytes 7864320 | tf_op jit(solution)/shard_map/all_gather | solution.py:42
  691.5 237.7 %reduce-scatter.12.cloned.1.call-start = ((), (), s32[]{:S(2)}) async-start(), calls=%async_computation.15 | async-start | bytes 15728640 | tf_op jit(solution)/shard_map/reduce_scatter | solution.py:46
  807.2 205.9 %all-gather.20.cloned.1.call-start = ((), (), s32[]{:S(2)}) async-start(), calls=%async_computation.16 | async-start | bytes 7864320 | tf_op jit(solution)/shard_map/all_gather | solution.py:42
  944.5 270.7 %reduce-scatter.20.cloned.1.call-start = ((), (), s32[]{:S(2)}) async-start(), calls=%async_computation.20 | async-start | bytes 4456448 | tf_op jit(solution)/shard_map/reduce_scatter | solution.py:229
  961.7 255.3 %reduce-scatter.18.cloned.1.call-start = ((), (), s32[]{:S(2)}) async-start(), calls=%async_computation.19 | async-start | bytes 4456448 | tf_op jit(solution)/shard_map/reduce_scatter | solution.py:226
  978.7 322.9 %all-reduce.5.cloned.1.call-start = ((), (), s32[]{:S(2)}) async-start(), calls=%async_computation.21 | async-start | bytes 8388608
  1189.8 172.0 %reduce-scatter.16.cloned.1.call-start = ((), (), s32[]{:S(2)}) async-start(), calls=%async_computation.18 | async-start | bytes 1114112 | tf_op jit(solution)/shard_map/reduce_scatter | solution.py:221
  1197.1 287.8 %reduce-scatter.14.cloned.1.call-start = ((), (), s32[]{:S(2)}) async-start(), calls=%async_computation.17 | async-start | bytes 15728640 | tf_op jit(solution)/shard_map/reduce_scatter | solution.py:46
  1213.2 271.6 %copy-start.2 = (bf16[1280,1024]{1,0:T(8,128)(2,1)S(1)}, bf16[1280,1024]{1,0:T(8,128)(2,1)}, u32[]{:S(2)}) copy-start(bf16[1280,1024]{1,0:T(8,128)(2,1)} %param.15) | copy-start | bytes 7864324
  1213.3 271.6 %copy-start.18 = (f32[1280]{0:T(1024)S(1)}, f32[1280]{0:T(1024)}, u32[]{:S(2)}) copy-start(f32[1280]{0:T(1024)} %copy-done.17) | copy-start | bytes 15364
  1213.3 271.6 %copy-start.29 = (f32[1024]{0:T(1024)S(1)}, f32[1024]{0:T(1024)}, u32[]{:S(2)}) copy-start(f32[1024]{0:T(1024)} %param.18) | copy-start | bytes 12292
  1216.9 271.8 %copy-start.27 = (f32[1280]{0:T(1024)S(1)}, f32[1280]{0:T(1024)}, u32[]{:S(2)}) copy-start(f32[1280]{0:T(1024)} %copy-done.26) | copy-start | bytes 15364
  1216.9 271.9 %copy-start.23 = (f32[1280]{0:T(1024)S(1)}, f32[1280]{0:T(1024)}, u32[]{:S(2)}) copy-start(f32[1280]{0:T(1024)} %copy-done.22) | copy-start | bytes 15364
  (44 other events, 1062.8 us)
Sparse Core Ops, SparseCore 0:
  14.8 71.2 all-gather.7
  88.2 55.3 all-gather.9
  243.5 122.5 reduce-scatter.7
  368.1 50.5 all-gather.13
  420.7 67.0 all-gather.11
  489.8 50.5 all-gather.15
  557.1 120.3 reduce-scatter.9
  691.6 68.5 all-gather.17
  807.4 121.8 reduce-scatter.11
  944.6 68.5 all-gather.19
  1017.0 72.3 reduce-scatter.19
  1093.6 71.8 reduce-scatter.17
  1190.0 111.5 all-reduce.4
  1305.5 56.2 reduce-scatter.15
  1363.9 120.8 reduce-scatter.13
